TPU v7x, 256 devices: a whole 4x4x8 slice. The times are simulated.
256 devices in a mesh: row: 16 (over y_lo, z), col: 16 (over x, y_hi, core).
Axes of the slice: x: 4, y: 4 (y_hi: 2, y_lo: 2; y = y_hi * 2 + y_lo), z: 8, core: 2. Of those that a mesh axis runs over, the one named last changes fastest.
Arguments:
- pair_rep: bfloat16 [512, 512, 128], P('row', 'col'), may hold values from -6 to 6
- residue_mask: int32 [512], replicated, may hold values 0 or 1
- input_weights: bfloat16 [2, 128, 512], replicated, may hold values from -0.5 to 0.5
- gate_weights: bfloat16 [2, 128, 128], replicated, may hold values from -0.5 to 0.5
- output_weights: bfloat16 [2, 128, 128], replicated, may hold values from -0.5 to 0.5
Outputs:
- updated_pair: bfloat16 [512, 512, 128], P('row', 'col')
All inputs are finite; a program needn't handle non-finite values.
Results may differ from a plain program's by a relative error of at most 0.0095.
Values may be sent and summed in bfloat16 or wider, within the bound.
A program may use at most 128 MiB of HBM per device.

v0:
```python
import functools

import jax
import jax.numpy as jnp
from jax import lax
from jax.experimental import pallas as pl
from jax.experimental.pallas import tpu as pltpu
from jax.sharding import PartitionSpec as P

EPS = 1e-05
MESH = pl.DeviceIdType.MESH
F32 = jnp.float32
BF16 = jnp.bfloat16


def sigmoid(x):
    return 0.5 * jnp.tanh(0.5 * x) + 0.5


def swap_blocks(parts):
    group = lax.broadcasted_iota(jnp.int32, parts[0].shape, parts[0].ndim - 1) // 32
    axis = parts[0].ndim - 1
    high = group >= 2
    odd = lax.rem(group, 2) == 1

    def far(a, b):
        c = pltpu.roll(jnp.where(high, a, b), 64, axis)
        return jnp.where(high, c, a), jnp.where(high, b, c)

    def near(a, b):
        c = jnp.where(odd, a, b)
        return jnp.where(odd, pltpu.roll(c, 32, axis), a), jnp.where(odd, b, pltpu.roll(c, 96, axis))

    p0, p2 = far(parts[0], parts[2])
    p1, p3 = far(parts[1], parts[3])
    p0, p1 = near(p0, p1)
    p2, p3 = near(p2, p3)
    return p0, p1, p2, p3


def far_first(step):
    pair, second = step // 2, lax.rem(step, 2)
    middle = (pair == 1) | (pair == 2)
    dx = jnp.where(middle, 1 + 2 * second, jnp.where(pair == 0, 2, 0))
    return dx, jnp.where(middle, 2 - pair, 1 - second)


ALONG_Z = ((4, 3), (2, 5), (6, 1), (0, 7))


def kernel(
    z_hbm, mask_hbm, win_hbm, wgate_hbm, wout_hbm, out_ref,
    zp, mask_ref, win, wgate, wout, normed, wt, mask8, gate,
    send1, recv1, left0, right0, left1, right1, send2, recv2,
    load, sem1s, sem1r, semxs, semxr, sem2s, sem2r, ready,
):
    r, c = lax.axis_index("row"), lax.axis_index("col")
    cc, core = c // 2, lax.rem(c, 2)
    y, z = r // 8, lax.rem(r, 8)
    x, yh = cc // 2, lax.rem(cc, 2)
    me = cc * 16 + r
    sibling = (r, cc * 2 + 1 - core)

    barrier = pltpu.get_barrier_semaphore()

    for dz in (4, 3, 5, 2, 6, 1, 7, 0):
        row = core * 8 + lax.rem(z + dz, 8)
        for k in range(2):
            far = lax.rem(x + 2, 4) * 4 + (1 - yh) * 2 + k
            pl.semaphore_signal(barrier, inc=1, device_id=(row, far), device_id_type=MESH)

    @pl.loop(1, 8)
    def _(t):
        peer = lax.rem(cc + t, 8) * 2 + core
        pl.semaphore_signal(barrier, inc=1, device_id=(r, peer), device_id_type=MESH)

    loads = [pltpu.make_async_copy(z_hbm.at[:, t], zp.at[t], load.at[t]) for t in range(8)]
    loads.append(pltpu.make_async_copy(win_hbm, win, load.at[8]))
    loads.append(pltpu.make_async_copy(wgate_hbm, wgate, load.at[9]))
    loads.append(pltpu.make_async_copy(wout_hbm, wout, load.at[10]))
    loads.append(pltpu.make_async_copy(mask_hbm, mask_ref, load.at[11]))
    for one in loads:
        one.start()

    loads[11].wait()
    valid = jnp.broadcast_to(mask_ref[...].astype(F32), (8, 512))
    n8 = lax.broadcasted_iota(jnp.int32, (8, 512), 1)
    t8 = lax.broadcasted_iota(jnp.int32, (8, 512), 0)
    n = lax.broadcasted_iota(jnp.int32, (512, 128), 0)
    l = lax.broadcasted_iota(jnp.int32, (512, 128), 1)
    rows = jnp.where(lax.rem(n8, 8) == t8, valid, 0.0).astype(BF16)
    pick_row = jnp.where(n // 8 == 4 * r + l // 32, 1.0, 0.0).astype(BF16)
    pick_col = jnp.where(n == 32 * c + lax.rem(l, 32), 1.0, 0.0).astype(BF16)
    mask8[...] = jnp.dot(rows, pick_row, preferred_element_type=F32) * jnp.dot(
        valid.astype(BF16), pick_col, preferred_element_type=F32
    )

    def normalize_rows(t, v):
        centred = v - jnp.mean(v, axis=-1, keepdims=True)
        variance = jnp.mean(centred * centred, axis=-1, keepdims=True)
        normed[pl.ds(t * 128, 128), :] = (centred * lax.rsqrt(variance + EPS)).astype(BF16)

    def turn_weights(u):
        for k in range(4):
            wt[u, k] = win[u, :, k * 128 : (k + 1) * 128].astype(F32).T.astype(BF16)

    def project(step, update):
        dx, dh = far_first(step)
        chip = lax.rem(x + dx, 4) * 2 + lax.rem(yh + dh, 2)
        at = pl.ds(pl.multiple_of(chip * 16, 16), 16)
        w = jnp.concatenate([wt[update, k, at, :] for k in range(4)], axis=0)
        p = lax.dot_general(w, normed[...], (((1,), (1,)), ((), ())), preferred_element_type=F32)
        both = []
        for k in (0, 32):
            side = sigmoid(p[k + 16 : k + 32]) * p[k : k + 16]
            tiles = jnp.stack([side[:, t * 128 : (t + 1) * 128] for t in range(8)], axis=0)
            both.append(jnp.swapaxes(tiles, 0, 1) * mask8[...][None])
        send1[update, at] = jnp.concatenate(both, axis=1).astype(BF16)

    for t in range(8):
        loads[t].wait()
        normalize_rows(t, zp[t].reshape(128, 128).astype(F32))
    loads[8].wait()
    turn_weights(0)

    for update in range(2):
        half = y if update == 0 else c // 8
        corner = lax.rem(c, 4)
        slot = x * 32 + z * 4 + corner if update == 0 else lax.rem(x, 2) * 64 + r * 4 + corner
        own = half == core

        def spread(step, update=update, half=half, own=own, slot=slot):
            dx, dh = far_first(step)
            chip = lax.rem(x + dx, 4) * 2 + lax.rem(yh + dh, 2)

            def send(row):
                pltpu.make_async_remote_copy(
                    src_ref=send1.at[update, chip * 16 + row],
                    dst_ref=recv1.at[update, slot],
                    send_sem=sem1s.at[update],
                    recv_sem=sem1r.at[update, dx],
                    device_id=(row, chip * 2 + half),
                    device_id_type=MESH,
                ).start()

            near = lax.rem(y + dh, 2)
            for parity, line in ((0, 1 - near), (0, near), (1, 1 - near), (1, near)):
                odd = lax.rem(parity + line + z + chip // 2 + chip, 2) == 1
                for way, dz in enumerate(ALONG_Z):
                    row = line * 8 + lax.rem(z + jnp.where(odd, dz[1], dz[0]), 8)
                    if way < 3 or line is not near:
                        send(row)
                        continue
                    here = (step == 7) & own & jnp.logical_not(odd)

                    @pl.when(jnp.logical_not(here))
                    def _(row=row):
                        send(row)

                    @pl.when(here)
                    def _():
                        pltpu.make_async_copy(
                            send1.at[update, me], recv1.at[update, slot], sem1r.at[update, dx]
                        ).start()

        if update == 0:
            project(0, 0)
            pl.semaphore_wait(barrier, 23)

            def tell(step, carry):
                dx, dh = far_first(step)
                peer = lax.rem(x + 6 - dx, 4) * 4 + lax.rem(1 + yh + dh, 2) * 2 + core
                pl.semaphore_signal(ready.at[step], inc=1, device_id=(r, peer), device_id_type=MESH)
                return carry

            lax.fori_loop(1, 8, tell, 0)
            spread(0)

            @pl.loop(1, 8)
            def _(step):
                project(step, 0)

            @pl.loop(1, 8)
            def _(step, spread=spread):
                pl.semaphore_wait(ready.at[step], 1)
                spread(step)

        else:

            @pl.loop(0, 8)
            def _(step, spread=spread):
                project(step, 1)
                spread(step)

        if update == 0:
            turn_weights(1)
            loads[9].wait()
            loads[10].wait()

        @pl.loop(0, 4)
        def _(i, update=update):
            at = pl.ds(pl.multiple_of(i * 256, 256), 256)
            gate[at, :] = sigmoid(jnp.dot(normed[at, :], wgate[update], preferred_element_type=F32))

        left, right = (left0, right0) if update == 0 else (left1, right1)
        columns = 4 if update == 0 else 2
        count = 128 // columns

        def arrive(dx, update=update, left=left, right=right, columns=columns, count=count):
            k = lax.rem(x + 4 - dx, columns)
            got = recv1.at[update, pl.ds(0, count)]
            pltpu.make_async_copy(got, got, sem1r.at[update, dx]).wait()
            for part in range(count // 32):
                at = pl.ds(part * 256, 256)
                v = recv1[update, pl.ds(k * count + part * 32, 32)].astype(F32).reshape(8, 4, 16, 128)
                parts = swap_blocks([v[:, q] for q in range(4)])
                for side in range(2):
                    rows = jnp.stack([p[:, side * 8 : side * 8 + 8] for p in parts], axis=1)
                    rows = rows.reshape(256, 128).astype(BF16)
                    if side == 0:
                        left[k, at, :] = rows
                    else:
                        right[core, k, at, :] = rows
            part = right.at[core, k]
            pltpu.make_async_remote_copy(
                src_ref=part, dst_ref=part, send_sem=semxs.at[update], recv_sem=semxr.at[update],
                device_id=sibling, device_id_type=MESH,
            ).start()

        if update == 0:

            def each(i, carry, arrive=arrive):
                arrive(jnp.where(i == 0, 2, jnp.where(i == 3, 0, 2 * i - 1)))
                return carry

            lax.fori_loop(0, 4, each, 0)
        else:
            ways = lax.rem(x + 4 - core * 2, 4)
            other = lax.rem(ways + 3, 4)
            even, odd = jnp.where(lax.rem(ways, 2) == 0, ways, other), jnp.where(lax.rem(ways, 2) == 0, other, ways)
            arrive(jnp.where(even == 2, even, odd))
            arrive(jnp.where(even == 2, odd, even))
        own_back = y == core
        way = lax.rem(core * 2 + 4 - x, 4)
        own_far = (way == 2) | (way == 1)
        own_odd = jnp.where(lax.rem(way, 2) == 1, way, lax.rem(way + 1, 4))

        def block_of(i, own_far=own_far, own_odd=own_odd):
            first = jnp.where(own_far, 2, own_odd)
            second = jnp.where(own_far, own_odd, 2)
            dx = jnp.where(i == 0, first, jnp.where(i == 1, second, jnp.where(i == 2, 4 - own_odd, 0)))
            return lax.rem(x + dx, 4)

        def back_sends(i, update=update, block_of=block_of, own_back=own_back):
            k = block_of(i)

            def send(col, b):
                pltpu.make_async_remote_copy(
                    src_ref=send2.at[update, col * 8 + b],
                    dst_ref=recv2.at[update, me],
                    send_sem=sem2s.at[update],
                    recv_sem=sem2r.at[update],
                    device_id=(core * 8 + b, col),
                    device_id_type=MESH,
                ).start()

            for parity, h in ((0, 1 - yh), (0, yh), (1, 1 - yh), (1, yh)):
                odd = lax.rem(parity + core + z + k + h, 2) == 1
                for way, dz in enumerate(ALONG_Z):
                    b = lax.rem(z + jnp.where(odd, dz[1], dz[0]), 8)
                    send(k * 4 + h * 2 + 1 - core, b)
                    if way < 3 or h is not yh:
                        send(k * 4 + h * 2 + core, b)
                        continue
                    here = (i == 3) & own_back & jnp.logical_not(odd)

                    @pl.when(jnp.logical_not(here))
                    def _(h=h, b=b):
                        send(k * 4 + h * 2 + core, b)

                    @pl.when(here)
                    def _():
                        pltpu.make_async_copy(
                            send2.at[update, c * 8 + z], recv2.at[update, me], sem2r.at[update]
                        ).start()

        def back(i, carry, update=update, left=left, right=right, block_of=block_of, back_sends=back_sends):
            k = block_of(i)
            if update == 0:
                some = pl.ds(pl.multiple_of(lax.rem(k, 2) * 128, 128), 128)
                lhs = jnp.concatenate([left[q] for q in range(4)], axis=1)
                rhs = jnp.concatenate([right[k // 2, q, some, :] for q in range(4)], axis=1)
                v = lax.dot_general(lhs, rhs, (((1,), (1,)), ((), ())), preferred_element_type=F32)
            else:
                lhs = jnp.concatenate([left[q] for q in range(2)], axis=1)
                rhs = right[k // 2, lax.rem(k, 2)]
                v = lax.dot_general(lhs, rhs, (((0,), (0,)), ((), ())), preferred_element_type=F32)
            v = v.reshape(8, 4, 8, 128)
            parts = swap_blocks([v[:, u] for u in range(4)])
            for q in range(4):
                send2[update, pl.ds((k * 4 + q) * 8, 8)] = parts[q].astype(BF16)

            back_sends(i)
            return carry

        back(0, 0)
        theirs = right.at[1 - core]
        pltpu.make_async_copy(theirs, theirs, semxr.at[update]).wait()
        lax.fori_loop(1, 4, back, 0)
        pltpu.make_async_copy(recv2.at[update], recv2.at[update], sem2r.at[update]).wait()

        tiles = jnp.swapaxes(recv2[update].astype(F32), 0, 1)
        for t in range(8):
            v = tiles[t]
            centred = v - jnp.mean(v, axis=0, keepdims=True)
            variance = jnp.mean(centred * centred, axis=0, keepdims=True)
            v = (centred * lax.rsqrt(variance + EPS)).astype(BF16)
            term = lax.dot_general(v, wout[update], (((0,), (0,)), ((), ())), preferred_element_type=F32)
            at = pl.ds(t * 128, 128)
            new = zp[t].reshape(128, 128).astype(F32) + gate[at, :] * term
            if update == 0:
                new = new.astype(BF16)
                zp[t] = new.reshape(4, 32, 128)
                normalize_rows(t, new.astype(F32))
            else:
                for u in range(4):
                    out_ref[u * 8 + t] = new[u * 32 : u * 32 + 32].astype(BF16)

        mine = right.at[core]
        pltpu.make_async_copy(mine, mine, semxs.at[update]).wait()
        for sent, sem, all_remote, count in (
            (send1, sem1s, jnp.logical_not(own), 128),
            (send2, sem2s, jnp.logical_not(own_back), 128),
        ):

            @pl.when(all_remote)
            def _(update=update, sent=sent, sem=sem):
                pltpu.make_async_copy(sent.at[update], sent.at[update], sem.at[update]).wait()

            @pl.when(jnp.logical_not(all_remote))
            def _(update=update, sent=sent, sem=sem, count=count):
                gone = sent.at[update, pl.ds(0, count - 1)]
                pltpu.make_async_copy(gone, gone, sem.at[update]).wait()


def per_device(pair_rep, residue_mask, input_weights, gate_weights, output_weights):
    vmem = pl.BlockSpec(memory_space=pltpu.VMEM)
    anywhere = pl.BlockSpec(memory_space=pl.ANY)
    dma = pltpu.SemaphoreType.DMA((2,))
    out = pl.pallas_call(
        kernel,
        out_shape=jax.ShapeDtypeStruct((32, 32, 128), BF16),
        in_specs=[anywhere] * 5,
        out_specs=vmem,
        scratch_shapes=[
            pltpu.VMEM((8, 4, 32, 128), BF16),
            pltpu.VMEM((1, 512), jnp.int32),
            pltpu.VMEM((2, 128, 512), BF16),
            pltpu.VMEM((2, 128, 128), BF16),
            pltpu.VMEM((2, 128, 128), BF16),
            pltpu.VMEM((1024, 128), BF16),
            pltpu.VMEM((2, 4, 128, 128), BF16),
            pltpu.VMEM((8, 128), F32),
            pltpu.VMEM((1024, 128), F32),
            pltpu.VMEM((2, 128, 16, 128), BF16),
            pltpu.VMEM((2, 128, 16, 128), BF16),
            pltpu.VMEM((4, 256, 128), BF16),
            pltpu.VMEM((2, 4, 256, 128), BF16),
            pltpu.VMEM((2, 512, 128), BF16),
            pltpu.VMEM((2, 2, 512, 128), BF16),
            pltpu.VMEM((2, 128, 8, 128), BF16),
            pltpu.VMEM((2, 128, 8, 128), BF16),
            pltpu.SemaphoreType.DMA((12,)),
            dma, pltpu.SemaphoreType.DMA((2, 4)), dma, dma, dma, dma,
            pltpu.SemaphoreType.REGULAR((8,)),
        ],
        compiler_params=pltpu.CompilerParams(
            collective_id=0, has_side_effects=True, vmem_limit_bytes=32 * 1024 * 1024
        ),
        name="triangles",
    )(
        pltpu.with_memory_space_constraint(pair_rep.reshape(4, 8, 32, 128), pltpu.HBM),
        pltpu.with_memory_space_constraint(residue_mask.reshape(1, 512), pltpu.HBM),
        pltpu.with_memory_space_constraint(input_weights, pltpu.HBM),
        pltpu.with_memory_space_constraint(gate_weights, pltpu.HBM),
        pltpu.with_memory_space_constraint(output_weights, pltpu.HBM),
    )
    return out


def solution(mesh):
    placed = (P("row", "col", None), P(), P(), P(), P())
    return jax.shard_map(
        per_device, mesh=mesh, in_specs=placed, out_specs=P("row", "col", None), check_vma=False
    )
```

profile of v0, /device:TPU:1, one launch (start us, length us, event | category | flops | bytes accessed | tf_op | source)
XLA Modules:
  0.0 67.0 jit_solution(9310162299924439746)
XLA Ops:
  0.0 66.3 %triangles.1 = bf16[32,32,128]{2,1,0:T(8,128)(2,1)S(1)} custom-call(bf16[4,8,32,128]{3,2,1,0:T(8,128)(2,1)} %bitcast.2, s32[1,512]{1,0:T(1,128)} %bitcast.3, bf16[2,128,512]{2,1,0:T(8,128)(2,1)} %win_hbm.1, bf16[2,128,128]{2,1,0:T(8,128)(2,1)} %wgate_hbm.1, bf16[2,128,128]{2,1,0:T(8,128)(2,1)} %wout_hbm.1), custom_call_target="tpu_custom_call" | custom-call | tf_op jit(solution)/shard_map/triangles/pallas_call | solution.py:350
  66.3 0.7 %copy.7 = bf16[32,32,128]{2,1,0:T(8,128)(2,1)} copy(bf16[32,32,128]{2,1,0:T(8,128)(2,1)S(1)} %triangles.1) | data formatting | bytes 524288
where the time goes:
time: 67.1 us; the launch traced here: 67 us
  Pallas kernels  66.3 us (99%)
  local copies, waits for them, and re-layouts  0.71 us (1%)
    pallas_call x1, Pallas kernels, per_device(): pl.pallas_call(kernel, out_shape=jax.ShapeDtypeStruct((32, 32, 128), BF16...  66.3 us

commit v1 on v0

--- a/solution.py
+++ b/solution.py
@@ -61,19 +61,6 @@
     me = cc * 16 + r
     sibling = (r, cc * 2 + 1 - core)
 
-    barrier = pltpu.get_barrier_semaphore()
-
-    for dz in (4, 3, 5, 2, 6, 1, 7, 0):
-        row = core * 8 + lax.rem(z + dz, 8)
-        for k in range(2):
-            far = lax.rem(x + 2, 4) * 4 + (1 - yh) * 2 + k
-            pl.semaphore_signal(barrier, inc=1, device_id=(row, far), device_id_type=MESH)
-
-    @pl.loop(1, 8)
-    def _(t):
-        peer = lax.rem(cc + t, 8) * 2 + core
-        pl.semaphore_signal(barrier, inc=1, device_id=(r, peer), device_id_type=MESH)
-
     loads = [pltpu.make_async_copy(z_hbm.at[:, t], zp.at[t], load.at[t]) for t in range(8)]
     loads.append(pltpu.make_async_copy(win_hbm, win, load.at[8]))
     loads.append(pltpu.make_async_copy(wgate_hbm, wgate, load.at[9]))
@@ -82,15 +69,28 @@
     for one in loads:
         one.start()
 
-    loads[11].wait()
-    valid = jnp.broadcast_to(mask_ref[...].astype(F32), (8, 512))
+    barrier = pltpu.get_barrier_semaphore()
+
+    for dz in (4, 3, 5, 2, 6, 1, 7, 0):
+        row = core * 8 + lax.rem(z + dz, 8)
+        for k in range(2):
+            far = lax.rem(x + 2, 4) * 4 + (1 - yh) * 2 + k
+            pl.semaphore_signal(barrier, inc=1, device_id=(row, far), device_id_type=MESH)
+
+    @pl.loop(1, 8)
+    def _(t):
+        peer = lax.rem(cc + t, 8) * 2 + core
+        pl.semaphore_signal(barrier, inc=1, device_id=(r, peer), device_id_type=MESH)
+
     n8 = lax.broadcasted_iota(jnp.int32, (8, 512), 1)
     t8 = lax.broadcasted_iota(jnp.int32, (8, 512), 0)
     n = lax.broadcasted_iota(jnp.int32, (512, 128), 0)
     l = lax.broadcasted_iota(jnp.int32, (512, 128), 1)
-    rows = jnp.where(lax.rem(n8, 8) == t8, valid, 0.0).astype(BF16)
     pick_row = jnp.where(n // 8 == 4 * r + l // 32, 1.0, 0.0).astype(BF16)
     pick_col = jnp.where(n == 32 * c + lax.rem(l, 32), 1.0, 0.0).astype(BF16)
+    loads[11].wait()
+    valid = jnp.broadcast_to(mask_ref[...].astype(F32), (8, 512))
+    rows = jnp.where(lax.rem(n8, 8) == t8, valid, 0.0).astype(BF16)
     mask8[...] = jnp.dot(rows, pick_row, preferred_element_type=F32) * jnp.dot(
         valid.astype(BF16), pick_col, preferred_element_type=F32
     )
@@ -177,11 +177,8 @@
             spread(0)
 
             @pl.loop(1, 8)
-            def _(step):
+            def _(step, spread=spread):
                 project(step, 0)
-
-            @pl.loop(1, 8)
-            def _(step, spread=spread):
                 pl.semaphore_wait(ready.at[step], 1)
                 spread(step)
 

time: 67.1 us -> 66.7 us (level)
  no operation moved by 1% of the time
where the time goes in v1:
time: 66.7 us; the launch traced here: 66.6 us
  Pallas kernels  65.9 us (99%)
  local copies, waits for them, and re-layouts  0.71 us (1%)
    pallas_call x1, Pallas kernels, per_device(): pl.pallas_call(kernel, out_shape=jax.ShapeDtypeStruct((32, 32, 128), BF16...  65.9 us

profile of v1, /device:TPU:1, one launch (start us, length us, event | category | flops | bytes accessed | tf_op | source)
XLA Modules:
  0.0 66.6 jit_solution(6748935127583499301)
XLA Ops:
  0.0 65.9 %triangles.1 = bf16[32,32,128]{2,1,0:T(8,128)(2,1)S(1)} custom-call(bf16[4,8,32,128]{3,2,1,0:T(8,128)(2,1)} %bitcast.2, s32[1,512]{1,0:T(1,128)} %bitcast.3, bf16[2,128,512]{2,1,0:T(8,128)(2,1)} %win_hbm.1, bf16[2,128,128]{2,1,0:T(8,128)(2,1)} %wgate_hbm.1, bf16[2,128,128]{2,1,0:T(8,128)(2,1)} %wout_hbm.1), custom_call_target="tpu_custom_call" | custom-call | tf_op jit(solution)/shard_map/triangles/pallas_call | solution.py:347
  65.9 0.7 %copy.7 = bf16[32,32,128]{2,1,0:T(8,128)(2,1)} copy(bf16[32,32,128]{2,1,0:T(8,128)(2,1)S(1)} %triangles.1) | data formatting | bytes 524288

commit v2 on v1

--- a/solution.py
+++ b/solution.py
@@ -117,8 +117,19 @@
             both.append(jnp.swapaxes(tiles, 0, 1) * mask8[...][None])
         send1[update, at] = jnp.concatenate(both, axis=1).astype(BF16)
 
+    def all_left(sent, sem, update, own):
+        @pl.when(own)
+        def _():
+            some = sent.at[update, pl.ds(0, 127)]
+            pltpu.make_async_copy(some, some, sem.at[update]).wait()
+
+        @pl.when(jnp.logical_not(own))
+        def _():
+            pltpu.make_async_copy(sent.at[update], sent.at[update], sem.at[update]).wait()
+
     for t in range(8):
         loads[t].wait()
+    for t in range(8):
         normalize_rows(t, zp[t].reshape(128, 128).astype(F32))
     loads[8].wait()
     turn_weights(0)
@@ -304,6 +315,9 @@
         theirs = right.at[1 - core]
         pltpu.make_async_copy(theirs, theirs, semxr.at[update]).wait()
         lax.fori_loop(1, 4, back, 0)
+        mine = right.at[core]
+        pltpu.make_async_copy(mine, mine, semxs.at[update]).wait()
+        all_left(send1, sem1s, update, own)
         pltpu.make_async_copy(recv2.at[update], recv2.at[update], sem2r.at[update]).wait()
 
         tiles = jnp.swapaxes(recv2[update].astype(F32), 0, 1)
@@ -323,21 +337,9 @@
                 for u in range(4):
                     out_ref[u * 8 + t] = new[u * 32 : u * 32 + 32].astype(BF16)
 
-        mine = right.at[core]
-        pltpu.make_async_copy(mine, mine, semxs.at[update]).wait()
-        for sent, sem, all_remote, count in (
-            (send1, sem1s, jnp.logical_not(own), 128),
-            (send2, sem2s, jnp.logical_not(own_back), 128),
-        ):
-
-            @pl.when(all_remote)
-            def _(update=update, sent=sent, sem=sem):
-                pltpu.make_async_copy(sent.at[update], sent.at[update], sem.at[update]).wait()
-
-            @pl.when(jnp.logical_not(all_remote))
-            def _(update=update, sent=sent, sem=sem, count=count):
-                gone = sent.at[update, pl.ds(0, count - 1)]
-                pltpu.make_async_copy(gone, gone, sem.at[update]).wait()
+    own_back = y == core
+    for update in range(2):
+        all_left(send2, sem2s, update, own_back)
 
 
 def per_device(pair_rep, residue_mask, input_weights, gate_weights, output_weights):

time: 66.7 us -> 66.7 us (level)
  no operation moved by 1% of the time
where the time goes in v2:
time: 66.7 us; the launch traced here: 66.6 us
  Pallas kernels  65.9 us (99%)
  local copies, waits for them, and re-layouts  0.71 us (1%)
    pallas_call x1, Pallas kernels, per_device(): pl.pallas_call(kernel, out_shape=jax.ShapeDtypeStruct((32, 32, 128), BF16...  65.9 us

profile of v2, /device:TPU:1, one launch (start us, length us, event | category | flops | bytes accessed | tf_op | source)
XLA Modules:
  0.0 66.6 jit_solution(1261841344838633509)
XLA Ops:
  0.0 65.9 %triangles.1 = bf16[32,32,128]{2,1,0:T(8,128)(2,1)S(1)} custom-call(bf16[4,8,32,128]{3,2,1,0:T(8,128)(2,1)} %bitcast.2, s32[1,512]{1,0:T(1,128)} %bitcast.3, bf16[2,128,512]{2,1,0:T(8,128)(2,1)} %win_hbm.1, bf16[2,128,128]{2,1,0:T(8,128)(2,1)} %wgate_hbm.1, bf16[2,128,128]{2,1,0:T(8,128)(2,1)} %wout_hbm.1), custom_call_target="tpu_custom_call" | custom-call | tf_op jit(solution)/shard_map/triangles/pallas_call | solution.py:349
  65.9 0.7 %copy.7 = bf16[32,32,128]{2,1,0:T(8,128)(2,1)} copy(bf16[32,32,128]{2,1,0:T(8,128)(2,1)S(1)} %triangles.1) | data formatting | bytes 524288

commit v3 on v1

--- a/solution.py
+++ b/solution.py
@@ -213,8 +213,13 @@
                 parts = swap_blocks([v[:, q] for q in range(4)])
                 for side in range(2):
                     rows = jnp.stack([p[:, side * 8 : side * 8 + 8] for p in parts], axis=1)
-                    rows = rows.reshape(256, 128).astype(BF16)
-                    if side == 0:
+                    rows = rows.reshape(256, 128)
+                    if side == 0 and update == 1:
+                        rows = rows.T
+                    rows = rows.astype(BF16)
+                    if side == 0 and update == 1:
+                        left[k, :, at] = rows
+                    elif side == 0:
                         left[k, at, :] = rows
                     else:
                         right[core, k, at, :] = rows
@@ -248,7 +253,7 @@
             dx = jnp.where(i == 0, first, jnp.where(i == 1, second, jnp.where(i == 2, 4 - own_odd, 0)))
             return lax.rem(x + dx, 4)
 
-        def back_sends(i, update=update, block_of=block_of, own_back=own_back):
+        def back_sends(i, rest, update=update, block_of=block_of, own_back=own_back):
             k = block_of(i)
 
             def send(col, b):
@@ -261,8 +266,8 @@
                     device_id_type=MESH,
                 ).start()
 
-            for parity, h in ((0, 1 - yh), (0, yh), (1, 1 - yh), (1, yh)):
-                odd = lax.rem(parity + core + z + k + h, 2) == 1
+            odd = lax.rem(rest + z, 2) == 1
+            for h in (1 - yh, yh):
                 for way, dz in enumerate(ALONG_Z):
                     b = lax.rem(z + jnp.where(odd, dz[1], dz[0]), 8)
                     send(k * 4 + h * 2 + 1 - core, b)
@@ -287,17 +292,18 @@
                 some = pl.ds(pl.multiple_of(lax.rem(k, 2) * 128, 128), 128)
                 lhs = jnp.concatenate([left[q] for q in range(4)], axis=1)
                 rhs = jnp.concatenate([right[k // 2, q, some, :] for q in range(4)], axis=1)
-                v = lax.dot_general(lhs, rhs, (((1,), (1,)), ((), ())), preferred_element_type=F32)
             else:
-                lhs = jnp.concatenate([left[q] for q in range(2)], axis=1)
+                lhs = jnp.concatenate([left[q] for q in range(2)], axis=0)
                 rhs = right[k // 2, lax.rem(k, 2)]
-                v = lax.dot_general(lhs, rhs, (((0,), (0,)), ((), ())), preferred_element_type=F32)
-            v = v.reshape(8, 4, 8, 128)
-            parts = swap_blocks([v[:, u] for u in range(4)])
-            for q in range(4):
-                send2[update, pl.ds((k * 4 + q) * 8, 8)] = parts[q].astype(BF16)
-
-            back_sends(i)
+            for rest in range(2):
+                rows = lhs.reshape(4, 2, 32, 512)[:, rest].reshape(128, 512)
+                v = lax.dot_general(rows, rhs, (((1,), (1 - update,)), ((), ())), preferred_element_type=F32)
+                v = v.reshape(4, 4, 8, 128)
+                parts = swap_blocks([v[:, u] for u in range(4)])
+                for q in range(4):
+                    for m in range(4):
+                        send2[update, (k * 4 + q) * 8 + m * 2 + rest] = parts[q][m].astype(BF16)
+                back_sends(i, rest)
             return carry
 
         back(0, 0)
@@ -363,7 +369,7 @@
             pltpu.VMEM((2, 128, 16, 128), BF16),
             pltpu.VMEM((4, 256, 128), BF16),
             pltpu.VMEM((2, 4, 256, 128), BF16),
-            pltpu.VMEM((2, 512, 128), BF16),
+            pltpu.VMEM((2, 128, 512), BF16),
             pltpu.VMEM((2, 2, 512, 128), BF16),
             pltpu.VMEM((2, 128, 8, 128), BF16),
             pltpu.VMEM((2, 128, 8, 128), BF16),

time: 66.7 us -> 66.6 us (level)
  no operation moved by 1% of the time
where the time goes in v3:
time: 66.6 us; the launch traced here: 66.5 us
  Pallas kernels  65.8 us (99%)
  local copies, waits for them, and re-layouts  0.71 us (1%)
    pallas_call x1, Pallas kernels, per_device(): pl.pallas_call(kernel, out_shape=jax.ShapeDtypeStruct((32, 32, 128), BF16...  65.8 us

profile of v3, /device:TPU:1, one launch (start us, length us, event | category | flops | bytes accessed | tf_op | source)
XLA Modules:
  0.0 66.5 jit_solution(5697341402473596594)
XLA Ops:
  0.0 65.8 %triangles.1 = bf16[32,32,128]{2,1,0:T(8,128)(2,1)S(1)} custom-call(bf16[4,8,32,128]{3,2,1,0:T(8,128)(2,1)} %bitcast.2, s32[1,512]{1,0:T(1,128)} %bitcast.3, bf16[2,128,512]{2,1,0:T(8,128)(2,1)} %win_hbm.1, bf16[2,128,128]{2,1,0:T(8,128)(2,1)} %wgate_hbm.1, bf16[2,128,128]{2,1,0:T(8,128)(2,1)} %wout_hbm.1), custom_call_target="tpu_custom_call" | custom-call | tf_op jit(solution)/shard_map/triangles/pallas_call | solution.py:353
  65.8 0.7 %copy.7 = bf16[32,32,128]{2,1,0:T(8,128)(2,1)} copy(bf16[32,32,128]{2,1,0:T(8,128)(2,1)S(1)} %triangles.1) | data formatting | bytes 524288
